TPU v7x, 32 devices: a whole 2x2x4 slice. The times are simulated.
32 devices in a mesh: tm: 4 (over z), height: 8 (over y, x, core).
Axes of the slice: x: 2, y: 2, z: 4, core: 2. Of those that a mesh axis runs over, the one named last changes fastest.
Arguments:
- latents: bfloat16 [9, 16, 128, 384], P(None, 'height', 'tm'), may hold values from -6 to 6
- gain_in: float32 [384], replicated, may hold values from 0.1 to 1.9
- weight_in: bfloat16 [3, 3, 3, 384, 384], replicated, may hold values from -0.0625 to 0.0625
- bias_in: float32 [384], replicated, may hold values from -3 to 3
- gain_mid: float32 [384], replicated, may hold values from 0.1 to 1.9
- weight_mid: bfloat16 [3, 3, 3, 384, 384], replicated, may hold values from -0.0625 to 0.0625
- bias_mid: float32 [384], replicated, may hold values from -2 to 2
- up_weight: bfloat16 [3, 3, 384, 192], replicated, may hold values from -0.109375 to 0.109375
- up_bias: float32 [192], replicated, may hold values from -2 to 2
Outputs:
- first_image: bfloat16 [32, 256, 192], P('height', 'tm')
- later_images: bfloat16 [8, 32, 256, 192], P('tm', 'height')
All inputs are finite; a program needn't handle non-finite values.
Results may differ from a plain program's by a relative error of at most 0.0053.
Values may be sent and summed in bfloat16 or wider, within the bound.
A program may use at most 128 MiB of HBM per device.

v0:
```python
import jax
import jax.numpy as jnp
from jax import lax
from jax.sharding import PartitionSpec as P

epsilon = 1e-06


def with_halo(array, sides, width):
    for axis, dim in sides:
        peers, length = (lax.axis_size(axis), array.shape[dim])
        up = [(i, (i + 1) % peers) for i in range(peers - 1)]
        down = [(j, i) for i, j in up]
        last = lax.slice_in_dim(array, length - width, length, axis=dim)
        leading = lax.slice_in_dim(array, 0, width, axis=dim)
        before = lax.ppermute(last, axis, up)
        after = lax.ppermute(leading, axis, down)
        array = jnp.concatenate([before, array, after], axis=dim)
    return array


def normed_silu(values, norm_gain):
    factor = lax.rsqrt(jnp.mean(values * values, axis=-1, keepdims=True) + epsilon)
    return jax.nn.silu(values * factor * norm_gain)


def column_pad(values):
    pad_spec = [(0, 0)] * (values.ndim - 2) + [(1, 1), (0, 0)]
    return jnp.pad(values, pad_spec)


def row_taps(slab_rows, tap_weights):
    col_count = slab_rows.shape[-2] - 2
    widened = jnp.concatenate(
        [slab_rows[..., offset : offset + col_count, :] for offset in range(3)], axis=-1
    )
    merged = tap_weights.reshape(3 * tap_weights.shape[1], tap_weights.shape[2])
    return jnp.einsum("...c,cd->...d", widened, merged, preferred_element_type=jnp.float32)


def plane_conv(padded, tap_weights):
    row_count = padded.shape[-3] - 2
    summed = row_taps(padded[..., 0:row_count, :, :], tap_weights[0])
    for offset in range(1, 3):
        summed = summed + row_taps(
            padded[..., offset : offset + row_count, :, :], tap_weights[offset]
        )
    return summed


def causal_conv(padded, weight):
    frame_count = padded.shape[0] - 2
    summed = plane_conv(padded[0:frame_count], weight[0])
    for offset in range(1, 3):
        summed = summed + plane_conv(padded[offset : offset + frame_count], weight[offset])
    return summed


def enlarge_conv(framed, tap_weights, col_start, col_count):
    doubled = jnp.repeat(jnp.repeat(framed, 2, axis=-3), 2, axis=-2)
    doubled = doubled[..., 1:-1, :, :]
    window = lax.dynamic_slice_in_dim(doubled, col_start + 1, col_count + 2, axis=doubled.ndim - 2)
    return plane_conv(window, tap_weights)


def brick_pad(values):
    rimmed = with_halo(values, (("tm", 2), ("height", 1)), 1)
    return jnp.pad(rimmed, ((2, 0), (0, 0), (0, 0), (0, 0)))


def body(latents, gain_in, weight_in, bias_in, gain_mid, weight_mid, bias_mid, up_weight, up_bias):
    groups = lax.axis_size("tm")
    frames_all, row_count, quarter, channels = latents.shape
    width_all = quarter * groups
    widened = latents.astype(jnp.float32)
    inner = normed_silu(widened, gain_in).astype(jnp.bfloat16)
    mixed = causal_conv(brick_pad(inner), weight_in) + bias_in
    middle = normed_silu(mixed, gain_mid).astype(jnp.bfloat16)
    result = causal_conv(brick_pad(middle), weight_mid) + bias_mid
    summed = (widened + result).astype(jnp.bfloat16)
    first_rimmed = with_halo(summed[0], (("tm", 1), ("height", 0)), 1)
    first_image = (enlarge_conv(first_rimmed, up_weight, 0, 2 * quarter) + up_bias).astype(
        jnp.bfloat16
    )
    later_block = lax.all_to_all(summed[1:], "tm", split_axis=0, concat_axis=2, tiled=True)
    later_in = column_pad(with_halo(later_block, (("height", 1),), 1))
    later_images = (enlarge_conv(later_in, up_weight, 0, 2 * width_all) + up_bias).astype(
        jnp.bfloat16
    )
    return (first_image, later_images)


def solution(mesh):
    return jax.shard_map(
        body,
        mesh=mesh,
        in_specs=(P(None, "height", "tm", None), P(), P(), P(), P(), P(), P(), P(), P()),
        out_specs=(P("height", "tm", None), P("tm", "height", None, None)),
        check_vma=False,
    )
```

profile of v0, /device:TPU:1, one launch (start us, length us, event | category | flops | bytes accessed | tf_op | source)
XLA Modules:
  0.0 134.4 jit_solution(5476568254930311724)
XLA Ops:
  3.2 4.0 %collective-permute-start = (bf16[9,2,1,384]{3,2,1,0:T(2,128)(2,1)S(1)}, bf16[9,2,1,384]{3,2,1,0:T(2,128)(2,1)S(1)}, u32[]{:S(2)}, u32[]{:S(2)}) collective-permute-start(bf16[9,2,1,384]{3,2,1,0:T(2,128)(2,1)S(1)} %get-tuple-element.90), channel_id=1, source_target_pairs={{0,8},{8,16},{16,24},{1,9},{9,17},{17,25},{2,10},{10,18},{18,26},{... | collective-permute-start | bytes 41480 | tf_op jit(solution)/shard_map/ppermute | solution.py:16
  8.6 3.8 %fusion.263 = (bf16[1,1,3,384,384]{4,3,2,1,0:T(8,128)(2,1)S(1)}, bf16[1,1,3,384,384]{4,3,2,1,0:T(8,128)(2,1)S(1)}, bf16[1,1,3,384,384]{4,3,2,1,0:T(8,128)(2,1)S(...) fusion(bf16[3,3,3,384,384]{4,3,2,1,0:T(8,128)(2,1)} %param.11), kind=kLoop, calls=%fused_computation.242 | loop fusion | bytes 15925248 | tf_op jit(solution)/shard_map/slice | solution.py:43
  12.8 4.6 %collective-permute-start.2 = (bf16[9,1,34,384]{3,2,1,0:T(8,128)(2,1)S(1)}, bf16[9,1,34,384]{3,2,1,0:T(8,128)(2,1)S(1)}, u32[]{:S(2)}, u32[]{:S(2)}) collective-permute-start(bf16[9,1,34,384]{3,2,1,0:T(8,128)(2,1)S(1)} %get-tuple-element.82), channel_id=1, source_target_pairs={{0,1},{1,2},{2,3},{3,4},{4,5},{5,6},{6,7},{8,9},{9,10},{10,11},{11... | collective-permute-start | bytes 705032 | tf_op jit(solution)/shard_map/ppermute | solution.py:16
  17.3 1.9 %collective-permute-start.3 = (bf16[9,1,34,384]{3,2,1,0:T(8,128)(2,1)S(1)}, bf16[9,1,34,384]{3,2,1,0:T(8,128)(2,1)S(1)}, u32[]{:S(2)}, u32[]{:S(2)}) collective-permute-start(bf16[9,1,34,384]{3,2,1,0:T(8,128)(2,1)S(1)} %get-tuple-element.83), channel_id=1, source_target_pairs={{1,0},{2,1},{3,2},{4,3},{5,4},{6,5},{7,6},{9,8},{10,9},{11,10},{12... | collective-permute-start | bytes 705032 | tf_op jit(solution)/shard_map/ppermute | solution.py:17
  20.8 4.6 %collective-permute-done.3 = bf16[9,1,34,384]{3,2,1,0:T(8,128)(2,1)S(1)} collective-permute-done((bf16[9,1,34,384]{3,2,1,0:T(8,128)(2,1)S(1)}, bf16[9,1,34,384]{3,2,1,0:T(8,128)(2,1)S(1)}, u32[]{:S(2)}, u32[]{:S(2)}) %collective-permute-start.3) | collective-permute-done | bytes 235040 | tf_op jit(solution)/shard_map/ppermute | solution.py:17
  25.7 1.8 %fusion.266 = (bf16[9,2,32,384]{3,2,1,0:T(8,128)(2,1)S(1)}, bf16[9,2,32,384]{3,2,1,0:T(8,128)(2,1)S(1)}, bf16[9,2,32,384]{3,2,1,0:T(8,128)(2,1)S(1)}, bf16[9,2,3...) fusion(bf16[11,4,34,384]{3,2,1,0:T(8,128)(2,1)S(1)} %fusion.33), kind=kLoop, calls=%fused_computation.245 | loop fusion | bytes 15925248 | tf_op jit(solution)/shard_map/slice | solution.py:35
  36.5 3.7 %collective-permute-start.4 = (bf16[9,2,1,384]{3,2,1,0:T(2,128)(2,1)S(1)}, bf16[9,2,1,384]{3,2,1,0:T(2,128)(2,1)S(1)}, u32[]{:S(2)}, u32[]{:S(2)}) collective-permute-start(bf16[9,2,1,384]{3,2,1,0:T(2,128)(2,1)S(1)} %get-tuple-element.88), channel_id=1, source_target_pairs={{0,8},{8,16},{16,24},{1,9},{9,17},{17,25},{2,10},{10,18},{18,26},{... | collective-permute-start | bytes 41480 | tf_op jit(solution)/shard_map/ppermute | solution.py:16
  42.6 2.1 %collective-permute-done.5 = bf16[9,2,1,384]{3,2,1,0:T(2,128)(2,1)S(1)} collective-permute-done((bf16[9,2,1,384]{3,2,1,0:T(2,128)(2,1)S(1)}, bf16[9,2,1,384]{3,2,1,0:T(2,128)(2,1)S(1)}, u32[]{:S(2)}, u32[]{:S(2)}) %collective-permute-start.5) | collective-permute-done | bytes 13856 | tf_op jit(solution)/shard_map/ppermute | solution.py:17
  45.1 3.2 %collective-permute-start.6 = (bf16[9,1,34,384]{3,2,1,0:T(8,128)(2,1)S(1)}, bf16[9,1,34,384]{3,2,1,0:T(8,128)(2,1)S(1)}, u32[]{:S(2)}, u32[]{:S(2)}) collective-permute-start(bf16[9,1,34,384]{3,2,1,0:T(8,128)(2,1)S(1)} %get-tuple-element.80), channel_id=1, source_target_pairs={{0,1},{1,2},{2,3},{3,4},{4,5},{5,6},{6,7},{8,9},{9,10},{10,11},{11... | collective-permute-start | bytes 705032 | tf_op jit(solution)/shard_map/ppermute | solution.py:16
  48.3 2.1 %collective-permute-start.7 = (bf16[9,1,34,384]{3,2,1,0:T(8,128)(2,1)S(1)}, bf16[9,1,34,384]{3,2,1,0:T(8,128)(2,1)S(1)}, u32[]{:S(2)}, u32[]{:S(2)}) collective-permute-start(bf16[9,1,34,384]{3,2,1,0:T(8,128)(2,1)S(1)} %get-tuple-element.81), channel_id=1, source_target_pairs={{1,0},{2,1},{3,2},{4,3},{5,4},{6,5},{7,6},{9,8},{10,9},{11,10},{12... | collective-permute-start | bytes 705032 | tf_op jit(solution)/shard_map/ppermute | solution.py:17
  51.7 5.3 %collective-permute-done.7 = bf16[9,1,34,384]{3,2,1,0:T(8,128)(2,1)S(1)} collective-permute-done((bf16[9,1,34,384]{3,2,1,0:T(8,128)(2,1)S(1)}, bf16[9,1,34,384]{3,2,1,0:T(8,128)(2,1)S(1)}, u32[]{:S(2)}, u32[]{:S(2)}) %collective-permute-start.7) | collective-permute-done | bytes 235040 | tf_op jit(solution)/shard_map/ppermute | solution.py:17
  67.4 3.2 %collective-permute-start.8 = (bf16[2,1,384]{2,1,0:T(2,128)(2,1)S(1)}, bf16[2,1,384]{2,1,0:T(2,128)(2,1)S(1)}, u32[]{:S(2)}, u32[]{:S(2)}) collective-permute-start(bf16[2,1,384]{2,1,0:T(2,128)(2,1)S(1)} %get-tuple-element.105), channel_id=1, source_target_pairs={{0,8},{8,16},{16,24},{1,9},{9,17},{17,25},{2,10},{10,18},{18,26},{... | collective-permute-start | bytes 4616 | tf_op jit(solution)/shard_map/ppermute | solution.py:16
  71.9 3.0 %collective-permute-done.9 = bf16[2,1,384]{2,1,0:T(2,128)(2,1)S(1)} collective-permute-done((bf16[2,1,384]{2,1,0:T(2,128)(2,1)S(1)}, bf16[2,1,384]{2,1,0:T(2,128)(2,1)S(1)}, u32[]{:S(2)}, u32[]{:S(2)}) %collective-permute-start.9) | collective-permute-done | bytes 1568 | tf_op jit(solution)/shard_map/ppermute | solution.py:17
  75.0 3.2 %collective-permute-start.10 = (bf16[1,34,384]{2,1,0:T(8,128)(2,1)S(1)}, bf16[1,34,384]{2,1,0:T(8,128)(2,1)S(1)}, u32[]{:S(2)}, u32[]{:S(2)}) collective-permute-start(bf16[1,34,384]{2,1,0:T(8,128)(2,1)S(1)} %get-tuple-element.103), channel_id=1, source_target_pairs={{0,1},{1,2},{2,3},{3,4},{4,5},{5,6},{6,7},{8,9},{9,10},{10,11},{11... | collective-permute-start | bytes 78344 | tf_op jit(solution)/shard_map/ppermute | solution.py:16
  78.2 1.9 %collective-permute-start.11 = (bf16[1,34,384]{2,1,0:T(8,128)(2,1)S(1)}, bf16[1,34,384]{2,1,0:T(8,128)(2,1)S(1)}, u32[]{:S(2)}, u32[]{:S(2)}) collective-permute-start(bf16[1,34,384]{2,1,0:T(8,128)(2,1)S(1)} %get-tuple-element.104), channel_id=1, source_target_pairs={{1,0},{2,1},{3,2},{4,3},{5,4},{6,5},{7,6},{9,8},{10,9},{11,10},{12... | collective-permute-start | bytes 78344 | tf_op jit(solution)/shard_map/ppermute | solution.py:17
  86.8 3.5 %all-to-all-start = ((bf16[8,2,32,384]{3,2,1,0:T(8,128)(2,1)}), bf16[8,2,32,384]{3,2,1,0:T(8,128)(2,1)S(1)}, u32[]{:S(2)}, u32[]{:S(2)}) async-start(bf16[8,2,32,384]{3,2,1,0:T(8,128)(2,1)} %slice.679), calls=%async_computation | async-start | bytes 786432 | tf_op jit(solution)/shard_map/all_to_all | solution.py:85
  91.7 9.6 %all-to-all-done = bf16[8,2,32,384]{3,2,1,0:T(8,128)(2,1)S(1)} async-done(((bf16[8,2,32,384]{3,2,1,0:T(8,128)(2,1)}), bf16[8,2,32,384]{3,2,1,0:T(8,128)(2,1)S(1)}, u32[]{:S(2)}, u32[]{:S(2)}) %all-to-all-start) | async-done | bytes 393248 | tf_op jit(solution)/shard_map/all_to_all | solution.py:85
  101.4 5.3 %collective-permute-start.12 = (bf16[2,1,128,384]{3,2,1,0:T(8,128)(2,1)S(1)}, bf16[2,1,128,384]{3,2,1,0:T(8,128)(2,1)S(1)}, u32[]{:S(2)}, u32[]{:S(2)}) collective-permute-start(bf16[2,1,128,384]{3,2,1,0:T(8,128)(2,1)S(1)} %get-tuple-element.92), channel_id=1, source_target_pairs={{0,1},{1,2},{2,3},{3,4},{4,5},{5,6},{6,7},{8,9},{9,10},{10,11},{11... | collective-permute-start | bytes 589832 | tf_op jit(solution)/shard_map/ppermute | solution.py:16
  106.7 2.1 %collective-permute-start.13 = (bf16[2,1,128,384]{3,2,1,0:T(8,128)(2,1)S(1)}, bf16[2,1,128,384]{3,2,1,0:T(8,128)(2,1)S(1)}, u32[]{:S(2)}, u32[]{:S(2)}) collective-permute-start(bf16[2,1,128,384]{3,2,1,0:T(8,128)(2,1)S(1)} %get-tuple-element.93), channel_id=1, source_target_pairs={{1,0},{2,1},{3,2},{4,3},{5,4},{6,5},{7,6},{9,8},{10,9},{11,10},{12... | collective-permute-start | bytes 589832 | tf_op jit(solution)/shard_map/ppermute | solution.py:17
  109.8 3.8 %collective-permute-done.13 = bf16[2,1,128,384]{3,2,1,0:T(8,128)(2,1)S(1)} collective-permute-done((bf16[2,1,128,384]{3,2,1,0:T(8,128)(2,1)S(1)}, bf16[2,1,128,384]{3,2,1,0:T(8,128)(2,1)S(1)}, u32[]{:S(2)}, u32[]{:S(2)}) %collective-permute-start.13) | collective-permute-done | bytes 196640 | tf_op jit(solution)/shard_map/ppermute | solution.py:17
  116.8 7.8 %fusion.264 = (bf16[2,4,256,384]{3,1,2,0:T(4,128)(2,1)S(1)}, bf16[2,4,256,384]{3,1,2,0:T(4,128)(2,1)S(1)}, bf16[2,4,256,384]{3,1,2,0:T(4,128)(2,1)S(1)}, bf16[2,...) fusion(bf16[2,8,260,384]{3,1,2,0:T(8,128)(2,1)S(1)} %bitcast.142), kind=kLoop, calls=%fused_computation.243 | loop fusion | bytes 28311552 | tf_op jit(solution)/shard_map/slice | solution.py:35
  127.2 2.2 %fusion.6 = f32[2,4,256,192]{2,3,1,0:T(8,128)S(1)} fusion(bf16[2,4,256,384]{3,2,1,0:T(8,128)(2,1)S(1)} %copy.54, bf16[2,4,256,384]{3,2,1,0:T(8,128)(2,1)S(1)} %copy.53, bf16[2,4,256,384]{3,2,1,0:T(8,128)(2,1)S(1)} %copy.52, bf16[1152,192,1,1]{0,1,2,3:T(8,128)(2,1)S(1)} %copy-done.4), kind=kOutput, calls=%fused_computation.6 | convolution fusion | flops 920125440 | bytes 6733824 | tf_op jit(solution)/shard_map/...c,cd->...d/dot_general | solution.py:38
  129.5 2.3 %fusion = f32[2,4,256,192]{2,3,1,0:T(8,128)S(1)} fusion(bf16[2,4,256,384]{3,2,1,0:T(8,128)(2,1)S(1)} %copy.51, bf16[2,4,256,384]{3,2,1,0:T(8,128)(2,1)S(1)} %copy.50, bf16[2,4,256,384]{3,2,1,0:T(8,128)(2,1)S(1)} %copy.49, bf16[1152,192,1,1]{0,1,2,3:T(8,128)(2,1)S(1)} %copy-done.2), kind=kOutput, calls=%fused_computation | convolution fusion | flops 920125440 | bytes 6733824 | tf_op jit(solution)/shard_map/...c,cd->...d/dot_general | solution.py:38
  131.8 2.7 %add_convert_fusion = bf16[2,4,256,192]{2,3,1,0:T(8,128)(2,1)} fusion(f32[2,4,256,192]{2,3,1,0:T(8,128)S(1)} %fusion, f32[2,4,256,192]{2,3,1,0:T(8,128)S(1)} %fusion.6, bf16[2,4,256,384]{3,2,1,0:T(8,128)(2,1)S(1)} %copy.57, bf16[2,4,256,384]{3,2,1,0:T(8,128)(2,1)S(1)} %copy.56, bf16[2,4,256,384]{3,2,1,0:T(8,128)(2,1)S(1)} %copy.55, f32[192]{0:T(256)S(1)} %copy-done.8, ...), kind=kOutput, calls=%fused_computation.29 | convolution fusion | flops 921698304 | bytes 9093888 | tf_op jit(solution)/shard_map/...c,cd->...d/dot_general | solution.py:38
  (114 shorter events, 45.3 us)
Async XLA Ops:
  3.2 9.2 %collective-permute-start = (bf16[9,2,1,384]{3,2,1,0:T(2,128)(2,1)S(1)}, bf16[9,2,1,384]{3,2,1,0:T(2,128)(2,1)S(1)}, u32[]{:S(2)}, u32[]{:S(2)}) collective-permute-start(bf16[9,2,1,384]{3,2,1,0:T(2,128)(2,1)S(1)} %get-tuple-element.90), channel_id=1, source_target_pairs={{0,8},{8,16},{16,24},{1,9},{9,17},{17,25},{2,10},{10,18},{18,26},{... | collective-permute-start | bytes 41480 | tf_op jit(solution)/shard_map/ppermute | solution.py:16
  7.3 5.1 %collective-permute-start.1 = (bf16[9,2,1,384]{3,2,1,0:T(2,128)(2,1)S(1)}, bf16[9,2,1,384]{3,2,1,0:T(2,128)(2,1)S(1)}, u32[]{:S(2)}, u32[]{:S(2)}) collective-permute-start(bf16[9,2,1,384]{3,2,1,0:T(2,128)(2,1)S(1)} %get-tuple-element.91), channel_id=1, source_target_pairs={{8,0},{16,8},{24,16},{9,1},{17,9},{25,17},{10,2},{18,10},{26,18},{... | collective-permute-start | bytes 41480 | tf_op jit(solution)/shard_map/ppermute | solution.py:17
  12.8 8.0 %collective-permute-start.2 = (bf16[9,1,34,384]{3,2,1,0:T(8,128)(2,1)S(1)}, bf16[9,1,34,384]{3,2,1,0:T(8,128)(2,1)S(1)}, u32[]{:S(2)}, u32[]{:S(2)}) collective-permute-start(bf16[9,1,34,384]{3,2,1,0:T(8,128)(2,1)S(1)} %get-tuple-element.82), channel_id=1, source_target_pairs={{0,1},{1,2},{2,3},{3,4},{4,5},{5,6},{6,7},{8,9},{9,10},{10,11},{11... | collective-permute-start | bytes 705032 | tf_op jit(solution)/shard_map/ppermute | solution.py:16
  17.3 8.1 %collective-permute-start.3 = (bf16[9,1,34,384]{3,2,1,0:T(8,128)(2,1)S(1)}, bf16[9,1,34,384]{3,2,1,0:T(8,128)(2,1)S(1)}, u32[]{:S(2)}, u32[]{:S(2)}) collective-permute-start(bf16[9,1,34,384]{3,2,1,0:T(8,128)(2,1)S(1)} %get-tuple-element.83), channel_id=1, source_target_pairs={{1,0},{2,1},{3,2},{4,3},{5,4},{6,5},{7,6},{9,8},{10,9},{11,10},{12... | collective-permute-start | bytes 705032 | tf_op jit(solution)/shard_map/ppermute | solution.py:17
  33.9 7.5 %slice-start = ((s8[7962624]{0:T(1024)(128)(4,1)}), s8[4194304]{0:T(1024)(128)(4,1)S(1)}, s32[]{:S(2)}) async-start(s8[7962624]{0:T(1024)(128)(4,1)} %bitcast.143), calls=%async_computation.1 | async-start | bytes 8388608
  34.0 7.5 %slice-start.1 = ((s8[7962624]{0:T(1024)(128)(4,1)}), s8[3768320]{0:T(1024)(128)(4,1)S(1)}, s32[]{:S(2)}) async-start(s8[7962624]{0:T(1024)(128)(4,1)} %bitcast.143), calls=%async_computation.2 | async-start | bytes 7536640
  34.9 1.2 copy-start.5
  36.5 6.1 %collective-permute-start.4 = (bf16[9,2,1,384]{3,2,1,0:T(2,128)(2,1)S(1)}, bf16[9,2,1,384]{3,2,1,0:T(2,128)(2,1)S(1)}, u32[]{:S(2)}, u32[]{:S(2)}) collective-permute-start(bf16[9,2,1,384]{3,2,1,0:T(2,128)(2,1)S(1)} %get-tuple-element.88), channel_id=1, source_target_pairs={{0,8},{8,16},{16,24},{1,9},{9,17},{17,25},{2,10},{10,18},{18,26},{... | collective-permute-start | bytes 41480 | tf_op jit(solution)/shard_map/ppermute | solution.py:16
  40.2 4.6 %collective-permute-start.5 = (bf16[9,2,1,384]{3,2,1,0:T(2,128)(2,1)S(1)}, bf16[9,2,1,384]{3,2,1,0:T(2,128)(2,1)S(1)}, u32[]{:S(2)}, u32[]{:S(2)}) collective-permute-start(bf16[9,2,1,384]{3,2,1,0:T(2,128)(2,1)S(1)} %get-tuple-element.89), channel_id=1, source_target_pairs={{8,0},{16,8},{24,16},{9,1},{17,9},{25,17},{10,2},{18,10},{26,18},{... | collective-permute-start | bytes 41480 | tf_op jit(solution)/shard_map/ppermute | solution.py:17
  45.1 6.6 %collective-permute-start.6 = (bf16[9,1,34,384]{3,2,1,0:T(8,128)(2,1)S(1)}, bf16[9,1,34,384]{3,2,1,0:T(8,128)(2,1)S(1)}, u32[]{:S(2)}, u32[]{:S(2)}) collective-permute-start(bf16[9,1,34,384]{3,2,1,0:T(8,128)(2,1)S(1)} %get-tuple-element.80), channel_id=1, source_target_pairs={{0,1},{1,2},{2,3},{3,4},{4,5},{5,6},{6,7},{8,9},{9,10},{10,11},{11... | collective-permute-start | bytes 705032 | tf_op jit(solution)/shard_map/ppermute | solution.py:16
  48.3 8.7 %collective-permute-start.7 = (bf16[9,1,34,384]{3,2,1,0:T(8,128)(2,1)S(1)}, bf16[9,1,34,384]{3,2,1,0:T(8,128)(2,1)S(1)}, u32[]{:S(2)}, u32[]{:S(2)}) collective-permute-start(bf16[9,1,34,384]{3,2,1,0:T(8,128)(2,1)S(1)} %get-tuple-element.81), channel_id=1, source_target_pairs={{1,0},{2,1},{3,2},{4,3},{5,4},{6,5},{7,6},{9,8},{10,9},{11,10},{12... | collective-permute-start | bytes 705032 | tf_op jit(solution)/shard_map/ppermute | solution.py:17
  65.3 1.0 copy-start
  66.3 13.8 %copy-start.1 = (bf16[3,3,384,192]{2,3,1,0:T(8,128)(2,1)S(1)}, bf16[3,3,384,192]{2,3,1,0:T(8,128)(2,1)}, u32[]{:S(2)}) copy-start(bf16[3,3,384,192]{2,3,1,0:T(8,128)(2,1)} %param.16) | copy-start | bytes 3981316
  67.4 4.5 %collective-permute-start.8 = (bf16[2,1,384]{2,1,0:T(2,128)(2,1)S(1)}, bf16[2,1,384]{2,1,0:T(2,128)(2,1)S(1)}, u32[]{:S(2)}, u32[]{:S(2)}) collective-permute-start(bf16[2,1,384]{2,1,0:T(2,128)(2,1)S(1)} %get-tuple-element.105), channel_id=1, source_target_pairs={{0,8},{8,16},{16,24},{1,9},{9,17},{17,25},{2,10},{10,18},{18,26},{... | collective-permute-start | bytes 4616 | tf_op jit(solution)/shard_map/ppermute | solution.py:16
  70.6 4.3 %collective-permute-start.9 = (bf16[2,1,384]{2,1,0:T(2,128)(2,1)S(1)}, bf16[2,1,384]{2,1,0:T(2,128)(2,1)S(1)}, u32[]{:S(2)}, u32[]{:S(2)}) collective-permute-start(bf16[2,1,384]{2,1,0:T(2,128)(2,1)S(1)} %get-tuple-element.106), channel_id=1, source_target_pairs={{8,0},{16,8},{24,16},{9,1},{17,9},{25,17},{10,2},{18,10},{26,18},{... | collective-permute-start | bytes 4616 | tf_op jit(solution)/shard_map/ppermute | solution.py:17
  75.0 15.3 %collective-permute-start.10 = (bf16[1,34,384]{2,1,0:T(8,128)(2,1)S(1)}, bf16[1,34,384]{2,1,0:T(8,128)(2,1)S(1)}, u32[]{:S(2)}, u32[]{:S(2)}) collective-permute-start(bf16[1,34,384]{2,1,0:T(8,128)(2,1)S(1)} %get-tuple-element.103), channel_id=1, source_target_pairs={{0,1},{1,2},{2,3},{3,4},{4,5},{5,6},{6,7},{8,9},{9,10},{10,11},{11... | collective-permute-start | bytes 78344 | tf_op jit(solution)/shard_map/ppermute | solution.py:16
  78.2 12.1 %collective-permute-start.11 = (bf16[1,34,384]{2,1,0:T(8,128)(2,1)S(1)}, bf16[1,34,384]{2,1,0:T(8,128)(2,1)S(1)}, u32[]{:S(2)}, u32[]{:S(2)}) collective-permute-start(bf16[1,34,384]{2,1,0:T(8,128)(2,1)S(1)} %get-tuple-element.104), channel_id=1, source_target_pairs={{1,0},{2,1},{3,2},{4,3},{5,4},{6,5},{7,6},{9,8},{10,9},{11,10},{12... | collective-permute-start | bytes 78344 | tf_op jit(solution)/shard_map/ppermute | solution.py:17
  86.8 14.4 %all-to-all-start = ((bf16[8,2,32,384]{3,2,1,0:T(8,128)(2,1)}), bf16[8,2,32,384]{3,2,1,0:T(8,128)(2,1)S(1)}, u32[]{:S(2)}, u32[]{:S(2)}) async-start(bf16[8,2,32,384]{3,2,1,0:T(8,128)(2,1)} %slice.679), calls=%async_computation | async-start | bytes 786432 | tf_op jit(solution)/shard_map/all_to_all | solution.py:85
  91.3 17.5 %copy-start.8 = (f32[192]{0:T(256)S(1)}, f32[192]{0:T(256)}, u32[]{:S(2)}) copy-start(f32[192]{0:T(256)} %param.17) | copy-start | bytes 2308
  101.4 8.5 %collective-permute-start.12 = (bf16[2,1,128,384]{3,2,1,0:T(8,128)(2,1)S(1)}, bf16[2,1,128,384]{3,2,1,0:T(8,128)(2,1)S(1)}, u32[]{:S(2)}, u32[]{:S(2)}) collective-permute-start(bf16[2,1,128,384]{3,2,1,0:T(8,128)(2,1)S(1)} %get-tuple-element.92), channel_id=1, source_target_pairs={{0,1},{1,2},{2,3},{3,4},{4,5},{5,6},{6,7},{8,9},{9,10},{10,11},{11... | collective-permute-start | bytes 589832 | tf_op jit(solution)/shard_map/ppermute | solution.py:16
  106.7 7.0 %collective-permute-start.13 = (bf16[2,1,128,384]{3,2,1,0:T(8,128)(2,1)S(1)}, bf16[2,1,128,384]{3,2,1,0:T(8,128)(2,1)S(1)}, u32[]{:S(2)}, u32[]{:S(2)}) collective-permute-start(bf16[2,1,128,384]{3,2,1,0:T(8,128)(2,1)S(1)} %get-tuple-element.93), channel_id=1, source_target_pairs={{1,0},{2,1},{3,2},{4,3},{5,4},{6,5},{7,6},{9,8},{10,9},{11,10},{12... | collective-permute-start | bytes 589832 | tf_op jit(solution)/shard_map/ppermute | solution.py:17
  126.2 1.0 copy-start.4
  127.2 2.2 %copy-start.2 = (bf16[1152,192,1,1]{0,1,2,3:T(8,128)(2,1)S(1)}, bf16[1152,192,1,1]{0,1,2,3:T(8,128)(2,1)}, u32[]{:S(2)}) copy-start(bf16[1152,192,1,1]{0,1,2,3:T(8,128)(2,1)} %reshape.97) | copy-start | bytes 1327108
  129.5 2.3 %copy-start.3 = (bf16[1152,192,1,1]{0,1,2,3:T(8,128)(2,1)S(1)}, bf16[1152,192,1,1]{0,1,2,3:T(8,128)(2,1)}, u32[]{:S(2)}) copy-start(bf16[1152,192,1,1]{0,1,2,3:T(8,128)(2,1)} %reshape.99) | copy-start | bytes 1327108
  (2 other events, 2.0 us)
where the time goes:
time: 135 us; the launch traced here: 134 us
  starting transfers between devices  42.5 us (31%)
  local copies, waits for them, and re-layouts  30.6 us (23%)
  waiting for transfers between devices  29.6 us (22%)
  matrix products  25.2 us (19%)
  other arithmetic  5.07 us (4%)
  between operations  1.5 us (1%)
    ppermute x7, starting transfers between devices, with_halo(): before = lax.ppermute(last, axis, up)  27.1 us
    dot_general x24, matrix products, row_taps(): jnp.einsum('...c,cd->...d', widened, merged, preferred_element_type=jnp.f...  25.2 us
    ppermute x7, waiting for transfers between devices, with_halo(): after = lax.ppermute(leading, axis, down)  18.9 us
    slice x7, local copies, waits for them, and re-layouts, row_taps(): slab_rows[..., offset:offset + col_count, :]  12.7 us
    ppermute x7, starting transfers between devices, with_halo(): after = lax.ppermute(leading, axis, down)  12 us
    all_to_all x1, waiting for transfers between devices, body(): lax.all_to_all(summed[1:], 'tm', split_axis=0, concat_axis=2, tiled=True)  9.57 us
    slice x3, local copies, waits for them, and re-layouts, plane_conv(): summed = row_taps(padded[..., 0:row_count, :, :], tap_weights[0])  5.34 us
    another operation x6, local copies, waits for them, and re-layouts, row_taps(): merged = tap_weights.reshape(3 * tap_weights.shape[1], tap_weights.shape[2])  4.56 us
  transfers between devices with their start and end apart: 15, of which 8 were waited for; matrix products, arithmetic and copies ran while one was open for 12% of the time, Pallas kernels for 0%

commit v1 on v0

--- a/solution.py
+++ b/solution.py
@@ -4,6 +4,12 @@
 from jax.sharding import PartitionSpec as P
 
 epsilon = 1e-06
+
+
+def exchange_blocks(x, axis, split, join):
+    pieces = jnp.split(x, lax.axis_size(axis), axis=split)
+    received = lax.all_to_all(jnp.stack(pieces), axis, 0, 0)
+    return jnp.concatenate(received, axis=join)
 
 
 def with_halo(array, sides, width):
@@ -82,7 +88,7 @@
     first_image = (enlarge_conv(first_rimmed, up_weight, 0, 2 * quarter) + up_bias).astype(
         jnp.bfloat16
     )
-    later_block = lax.all_to_all(summed[1:], "tm", split_axis=0, concat_axis=2, tiled=True)
+    later_block = exchange_blocks(summed[1:], "tm", 0, 2)
     later_in = column_pad(with_halo(later_block, (("height", 1),), 1))
     later_images = (enlarge_conv(later_in, up_weight, 0, 2 * width_all) + up_bias).astype(
         jnp.bfloat16

time: 135 us -> 141 us (1.044)
  local copies, waits for them, and re-layouts: 30.6 us -> 37.4 us
  waiting for transfers between devices: 29.6 us -> 26.7 us
    unnamed x32 -> x52, local copies, waits for them, and re-layouts: 3.37 us -> 6.72 us
    slice x3, local copies, waits for them, and re-layouts: 5.34 us -> 7.84 us  [plane_conv(): summed = row_taps(padded[..., 0:row_count, :, :], tap_weights[0])]
    ppermute x7, waiting for transfers between devices: 18.9 us -> 16.7 us  [with_halo(): after = lax.ppermute(leading, axis, down)]
    another operation x6, local copies, waits for them, and re-layouts: 4.56 us -> 6.24 us  [row_taps(): merged = tap_weights.reshape(3 * tap_weights.shape[1], tap_weights.shape[2])]
  transfers between devices with their start and end apart: 15 -> 15, of which waited for: 8 -> 7; matrix products, arithmetic and copies ran while one was open for 12% -> 14% of each run, Pallas kernels for 0% -> 0%
where the time goes in v1:
time: 141 us; the launch traced here: 140 us
  starting transfers between devices  43 us (30%)
  local copies, waits for them, and re-layouts  37.4 us (27%)
  waiting for transfers between devices  26.7 us (19%)
  matrix products  25.1 us (18%)
  other arithmetic  6.05 us (4%)
  between operations  1.51 us (1%)
    ppermute x7, starting transfers between devices, with_halo(): before = lax.ppermute(last, axis, up)  26.8 us
    dot_general x24, matrix products, row_taps(): jnp.einsum('...c,cd->...d', widened, merged, preferred_element_type=jnp.f...  25.1 us
    ppermute x7, waiting for transfers between devices, with_halo(): after = lax.ppermute(leading, axis, down)  16.7 us
    slice x7, local copies, waits for them, and re-layouts, row_taps(): slab_rows[..., offset:offset + col_count, :]  12.7 us
    ppermute x7, starting transfers between devices, with_halo(): after = lax.ppermute(leading, axis, down)  12.6 us
    all_to_all x1, waiting for transfers between devices, exchange_blocks(): received = lax.all_to_all(jnp.stack(pieces), axis, 0, 0)  9.13 us
    slice x3, local copies, waits for them, and re-layouts, plane_conv(): summed = row_taps(padded[..., 0:row_count, :, :], tap_weights[0])  7.84 us
    unnamed x52, local copies, waits for them, and re-layouts  6.72 us
  transfers between devices with their start and end apart: 15, of which 7 were waited for; matrix products, arithmetic and copies ran while one was open for 14% of the time, Pallas kernels for 0%

profile of v1, /device:TPU:1, one launch (start us, length us, event | category | flops | bytes accessed | tf_op | source)
XLA Modules:
  0.0 139.7 jit_solution(702861016025706970)
XLA Ops:
  3.4 4.0 %collective-permute-start = (bf16[9,2,1,384]{3,2,1,0:T(2,128)(2,1)S(1)}, bf16[9,2,1,384]{3,2,1,0:T(2,128)(2,1)S(1)}, u32[]{:S(2)}, u32[]{:S(2)}) collective-permute-start(bf16[9,2,1,384]{3,2,1,0:T(2,128)(2,1)S(1)} %get-tuple-element.94), channel_id=1, source_target_pairs={{0,8},{8,16},{16,24},{1,9},{9,17},{17,25},{2,10},{10,18},{18,26},{... | collective-permute-start | bytes 41480 | tf_op jit(solution)/shard_map/ppermute | solution.py:22
  9.0 4.0 %fusion.263 = (bf16[1,1,3,384,384]{4,3,2,1,0:T(8,128)(2,1)S(1)}, bf16[1,1,3,384,384]{4,3,2,1,0:T(8,128)(2,1)S(1)}, bf16[1,1,3,384,384]{4,3,2,1,0:T(8,128)(2,1)S(...) fusion(bf16[3,3,3,384,384]{4,3,2,1,0:T(8,128)(2,1)} %param.11), kind=kLoop, calls=%fused_computation.247 | loop fusion | bytes 15925248 | tf_op jit(solution)/shard_map/slice | solution.py:49
  13.1 3.5 %fusion.262 = (bf16[1,1,3,384,384]{4,3,2,1,0:T(8,128)(2,1)S(1)}, bf16[1,1,3,384,384]{4,3,2,1,0:T(8,128)(2,1)}, bf16[1,1,3,384,384]{4,3,2,1,0:T(8,128)(2,1)}, bf1...) fusion(bf16[3,3,3,384,384]{4,3,2,1,0:T(8,128)(2,1)S(1)} %bitcas, ...), kind=kLoop, calls=%fused_computation.246 | loop fusion | bytes 15925248 | tf_op jit(solution)/shard_map/slice | solution.py:49
  16.9 4.0 %collective-permute-start.2 = (bf16[9,1,34,384]{3,2,1,0:T(8,128)(2,1)S(1)}, bf16[9,1,34,384]{3,2,1,0:T(8,128)(2,1)S(1)}, u32[]{:S(2)}, u32[]{:S(2)}) collective-permute-start(bf16[9,1,34,384]{3,2,1,0:T(8,128)(2,1)S(1)} %get-tuple-element.82), channel_id=1, source_target_pairs={{0,1},{1,2},{2,3},{3,4},{4,5},{5,6},{6,7},{8,9},{9,10},{10,11},{11... | collective-permute-start | bytes 705032 | tf_op jit(solution)/shard_map/ppermute | solution.py:22
  20.8 1.9 %collective-permute-start.3 = (bf16[9,1,34,384]{3,2,1,0:T(8,128)(2,1)S(1)}, bf16[9,1,34,384]{3,2,1,0:T(8,128)(2,1)S(1)}, u32[]{:S(2)}, u32[]{:S(2)}) collective-permute-start(bf16[9,1,34,384]{3,2,1,0:T(8,128)(2,1)S(1)} %get-tuple-element.83), channel_id=1, source_target_pairs={{1,0},{2,1},{3,2},{4,3},{5,4},{6,5},{7,6},{9,8},{10,9},{11,10},{12... | collective-permute-start | bytes 705032 | tf_op jit(solution)/shard_map/ppermute | solution.py:23
  24.3 4.6 %collective-permute-done.3 = bf16[9,1,34,384]{3,2,1,0:T(8,128)(2,1)S(1)} collective-permute-done((bf16[9,1,34,384]{3,2,1,0:T(8,128)(2,1)S(1)}, bf16[9,1,34,384]{3,2,1,0:T(8,128)(2,1)S(1)}, u32[]{:S(2)}, u32[]{:S(2)}) %collective-permute-start.3) | collective-permute-done | bytes 235040 | tf_op jit(solution)/shard_map/ppermute | solution.py:23
  39.8 4.3 %collective-permute-start.4 = (bf16[9,2,1,384]{3,2,1,0:T(2,128)(2,1)S(1)}, bf16[9,2,1,384]{3,2,1,0:T(2,128)(2,1)S(1)}, u32[]{:S(2)}, u32[]{:S(2)}) collective-permute-start(bf16[9,2,1,384]{3,2,1,0:T(2,128)(2,1)S(1)} %get-tuple-element.92), channel_id=1, source_target_pairs={{0,8},{8,16},{16,24},{1,9},{9,17},{17,25},{2,10},{10,18},{18,26},{... | collective-permute-start | bytes 41480 | tf_op jit(solution)/shard_map/ppermute | solution.py:22
  53.5 2.0 %collective-permute-start.6 = (bf16[9,1,34,384]{3,2,1,0:T(8,128)(2,1)S(1)}, bf16[9,1,34,384]{3,2,1,0:T(8,128)(2,1)S(1)}, u32[]{:S(2)}, u32[]{:S(2)}) collective-permute-start(bf16[9,1,34,384]{3,2,1,0:T(8,128)(2,1)S(1)} %get-tuple-element.80), channel_id=1, source_target_pairs={{0,1},{1,2},{2,3},{3,4},{4,5},{5,6},{6,7},{8,9},{9,10},{10,11},{11... | collective-permute-start | bytes 705032 | tf_op jit(solution)/shard_map/ppermute | solution.py:22
  55.5 2.3 %collective-permute-start.7 = (bf16[9,1,34,384]{3,2,1,0:T(8,128)(2,1)S(1)}, bf16[9,1,34,384]{3,2,1,0:T(8,128)(2,1)S(1)}, u32[]{:S(2)}, u32[]{:S(2)}) collective-permute-start(bf16[9,1,34,384]{3,2,1,0:T(8,128)(2,1)S(1)} %get-tuple-element.81), channel_id=1, source_target_pairs={{1,0},{2,1},{3,2},{4,3},{5,4},{6,5},{7,6},{9,8},{10,9},{11,10},{12... | collective-permute-start | bytes 705032 | tf_op jit(solution)/shard_map/ppermute | solution.py:23
  59.0 5.3 %collective-permute-done.7 = bf16[9,1,34,384]{3,2,1,0:T(8,128)(2,1)S(1)} collective-permute-done((bf16[9,1,34,384]{3,2,1,0:T(8,128)(2,1)S(1)}, bf16[9,1,34,384]{3,2,1,0:T(8,128)(2,1)S(1)}, u32[]{:S(2)}, u32[]{:S(2)}) %collective-permute-start.7) | collective-permute-done | bytes 235040 | tf_op jit(solution)/shard_map/ppermute | solution.py:23
  64.6 1.8 %fusion.265 = (bf16[9,2,32,384]{3,2,1,0:T(8,128)(2,1)S(1)}, bf16[9,2,32,384]{3,2,1,0:T(8,128)(2,1)S(1)}, bf16[9,2,32,384]{3,2,1,0:T(8,128)(2,1)S(1)}, bf16[9,2,3...) fusion(bf16[11,4,34,384]{3,2,1,0:T(8,128)(2,1)S(1)} %fusion.31), kind=kLoop, calls=%fused_computation.249 | loop fusion | bytes 15925248 | tf_op jit(solution)/shard_map/slice | solution.py:41
  77.3 4.3 %collective-permute-start.8 = (bf16[2,1,384]{2,1,0:T(2,128)(2,1)S(1)}, bf16[2,1,384]{2,1,0:T(2,128)(2,1)S(1)}, u32[]{:S(2)}, u32[]{:S(2)}) collective-permute-start(bf16[2,1,384]{2,1,0:T(2,128)(2,1)S(1)} %get-tuple-element.109), channel_id=1, source_target_pairs={{0,8},{8,16},{16,24},{1,9},{9,17},{17,25},{2,10},{10,18},{18,26},{... | collective-permute-start | bytes 4616 | tf_op jit(solution)/shard_map/ppermute | solution.py:22
  83.0 3.0 %collective-permute-done.9 = bf16[2,1,384]{2,1,0:T(2,128)(2,1)S(1)} collective-permute-done((bf16[2,1,384]{2,1,0:T(2,128)(2,1)S(1)}, bf16[2,1,384]{2,1,0:T(2,128)(2,1)S(1)}, u32[]{:S(2)}, u32[]{:S(2)}) %collective-permute-start.9) | collective-permute-done | bytes 1568 | tf_op jit(solution)/shard_map/ppermute | solution.py:23
  86.0 3.2 %collective-permute-start.10 = (bf16[1,34,384]{2,1,0:T(8,128)(2,1)S(1)}, bf16[1,34,384]{2,1,0:T(8,128)(2,1)S(1)}, u32[]{:S(2)}, u32[]{:S(2)}) collective-permute-start(bf16[1,34,384]{2,1,0:T(8,128)(2,1)S(1)} %get-tuple-element.107), channel_id=1, source_target_pairs={{0,1},{1,2},{2,3},{3,4},{4,5},{5,6},{6,7},{8,9},{9,10},{10,11},{11... | collective-permute-start | bytes 78344 | tf_op jit(solution)/shard_map/ppermute | solution.py:22
  89.2 1.9 %collective-permute-start.11 = (bf16[1,34,384]{2,1,0:T(8,128)(2,1)S(1)}, bf16[1,34,384]{2,1,0:T(8,128)(2,1)S(1)}, u32[]{:S(2)}, u32[]{:S(2)}) collective-permute-start(bf16[1,34,384]{2,1,0:T(8,128)(2,1)S(1)} %get-tuple-element.108), channel_id=1, source_target_pairs={{1,0},{2,1},{3,2},{4,3},{5,4},{6,5},{7,6},{9,8},{10,9},{11,10},{12... | collective-permute-start | bytes 78344 | tf_op jit(solution)/shard_map/ppermute | solution.py:23
  91.9 3.6 %all-to-all-start = ((bf16[4,2,2,32,384]{4,3,2,1,0:T(8,128)(2,1)}), bf16[4,2,2,32,384]{4,3,2,1,0:T(8,128)(2,1)S(1)}, u32[]{:S(2)}, u32[]{:S(2)}) async-start(bf16[4,2,2,32,384]{4,3,2,1,0:T(8,128)(2,1)} %pad_maximum_fusion.9), calls=%async_computation | async-start | bytes 786432 | tf_op jit(solution)/shard_map/all_to_all | solution.py:11
  97.7 9.1 %all-to-all-done = bf16[4,2,2,32,384]{4,3,2,1,0:T(8,128)(2,1)S(1)} async-done(((bf16[4,2,2,32,384]{4,3,2,1,0:T(8,128)(2,1)}), bf16[4,2,2,32,384]{4,3,2,1,0:T(8,128)(2,1)S(1)}, u32[]{:S(2)}, u32[]{:S(2)}) %all-to-all-start) | async-done | bytes 393248 | tf_op jit(solution)/shard_map/all_to_all | solution.py:11
  106.9 5.0 %collective-permute-start.12 = (bf16[2,1,128,384]{3,2,1,0:T(8,128)(2,1)S(1)}, bf16[2,1,128,384]{3,2,1,0:T(8,128)(2,1)S(1)}, u32[]{:S(2)}, u32[]{:S(2)}) collective-permute-start(bf16[2,1,128,384]{3,2,1,0:T(8,128)(2,1)S(1)} %get-tuple-element.96), channel_id=1, source_target_pairs={{0,1},{1,2},{2,3},{3,4},{4,5},{5,6},{6,7},{8,9},{9,10},{10,11},{11... | collective-permute-start | bytes 589832 | tf_op jit(solution)/shard_map/ppermute | solution.py:22
  112.0 2.1 %collective-permute-start.13 = (bf16[2,1,128,384]{3,2,1,0:T(8,128)(2,1)S(1)}, bf16[2,1,128,384]{3,2,1,0:T(8,128)(2,1)S(1)}, u32[]{:S(2)}, u32[]{:S(2)}) collective-permute-start(bf16[2,1,128,384]{3,2,1,0:T(8,128)(2,1)S(1)} %get-tuple-element.97), channel_id=1, source_target_pairs={{1,0},{2,1},{3,2},{4,3},{5,4},{6,5},{7,6},{9,8},{10,9},{11,10},{12... | collective-permute-start | bytes 589832 | tf_op jit(solution)/shard_map/ppermute | solution.py:23
  115.1 3.8 %collective-permute-done.13 = bf16[2,1,128,384]{3,2,1,0:T(8,128)(2,1)S(1)} collective-permute-done((bf16[2,1,128,384]{3,2,1,0:T(8,128)(2,1)S(1)}, bf16[2,1,128,384]{3,2,1,0:T(8,128)(2,1)S(1)}, u32[]{:S(2)}, u32[]{:S(2)}) %collective-permute-start.13) | collective-permute-done | bytes 196640 | tf_op jit(solution)/shard_map/ppermute | solution.py:23
  122.0 7.8 %fusion.264 = (bf16[2,4,256,384]{3,1,2,0:T(4,128)(2,1)S(1)}, bf16[2,4,256,384]{3,1,2,0:T(4,128)(2,1)S(1)}, bf16[2,4,256,384]{3,1,2,0:T(4,128)(2,1)S(1)}, bf16[2,...) fusion(bf16[2,8,260,384]{3,1,2,0:T(8,128)(2,1)S(1)} %bitcast.148), kind=kLoop, calls=%fused_computation.248 | loop fusion | bytes 28311552 | tf_op jit(solution)/shard_map/slice | solution.py:41
  132.5 2.2 %fusion.6 = f32[2,4,256,192]{2,3,1,0:T(8,128)S(1)} fusion(bf16[2,4,256,384]{3,2,1,0:T(8,128)(2,1)S(1)} %copy.54, bf16[2,4,256,384]{3,2,1,0:T(8,128)(2,1)S(1)} %copy.53, bf16[2,4,256,384]{3,2,1,0:T(8,128)(2,1)S(1)} %copy.52, bf16[1152,192,1,1]{0,1,2,3:T(8,128)(2,1)S(1)} %copy-done.12), kind=kOutput, calls=%fused_computation.6 | convolution fusion | flops 920125440 | bytes 6733824 | tf_op jit(solution)/shard_map/...c,cd->...d/dot_general | solution.py:44
  134.8 2.3 %fusion = f32[2,4,256,192]{2,3,1,0:T(8,128)S(1)} fusion(bf16[2,4,256,384]{3,2,1,0:T(8,128)(2,1)S(1)} %copy.51, bf16[2,4,256,384]{3,2,1,0:T(8,128)(2,1)S(1)} %copy.50, bf16[2,4,256,384]{3,2,1,0:T(8,128)(2,1)S(1)} %copy.49, bf16[1152,192,1,1]{0,1,2,3:T(8,128)(2,1)S(1)} %copy-done.10), kind=kOutput, calls=%fused_computation | convolution fusion | flops 920125440 | bytes 6733824 | tf_op jit(solution)/shard_map/...c,cd->...d/dot_general | solution.py:44
  137.0 2.7 %add_convert_fusion = bf16[2,4,256,192]{2,3,1,0:T(8,128)(2,1)} fusion(f32[2,4,256,192]{2,3,1,0:T(8,128)S(1)} %fusion, f32[2,4,256,192]{2,3,1,0:T(8,128)S(1)} %fusion.6, bf16[2,4,256,384]{3,2,1,0:T(8,128)(2,1)S(1)} %copy.57, bf16[2,4,256,384]{3,2,1,0:T(8,128)(2,1)S(1)} %copy.56, bf16[2,4,256,384]{3,2,1,0:T(8,128)(2,1)S(1)} %copy.55, f32[192]{0:T(256)S(1)} %copy-done.18, ...), kind=kOutput, calls=%fused_computation.29 | convolution fusion | flops 921698304 | bytes 9093888 | tf_op jit(solution)/shard_map/...c,cd->...d/dot_general | solution.py:44
  (135 shorter events, 49.6 us)
Async XLA Ops:
  1.8 11.2 %slice-start = ((s8[7962624]{0:T(1024)(128)(4,1)}), s8[4194304]{0:T(1024)(128)(4,1)S(1)}, s32[]{:S(2)}) async-start(s8[7962624]{0:T(1024)(128)(4,1)} %bitcast.149), calls=%async_computation.1 | async-start | bytes 8388608
  3.4 13.1 %collective-permute-start = (bf16[9,2,1,384]{3,2,1,0:T(2,128)(2,1)S(1)}, bf16[9,2,1,384]{3,2,1,0:T(2,128)(2,1)S(1)}, u32[]{:S(2)}, u32[]{:S(2)}) collective-permute-start(bf16[9,2,1,384]{3,2,1,0:T(2,128)(2,1)S(1)} %get-tuple-element.94), channel_id=1, source_target_pairs={{0,8},{8,16},{16,24},{1,9},{9,17},{17,25},{2,10},{10,18},{18,26},{... | collective-permute-start | bytes 41480 | tf_op jit(solution)/shard_map/ppermute | solution.py:22
  7.4 5.6 %slice-start.1 = ((s8[7962624]{0:T(1024)(128)(4,1)}), s8[3768320]{0:T(1024)(128)(4,1)S(1)}, s32[]{:S(2)}) async-start(s8[7962624]{0:T(1024)(128)(4,1)} %bitcast.149), calls=%async_computation.2 | async-start | bytes 7536640
  7.5 9.1 %collective-permute-start.1 = (bf16[9,2,1,384]{3,2,1,0:T(2,128)(2,1)S(1)}, bf16[9,2,1,384]{3,2,1,0:T(2,128)(2,1)S(1)}, u32[]{:S(2)}, u32[]{:S(2)}) collective-permute-start(bf16[9,2,1,384]{3,2,1,0:T(2,128)(2,1)S(1)} %get-tuple-element.95), channel_id=1, source_target_pairs={{8,0},{16,8},{24,16},{9,1},{17,9},{25,17},{10,2},{18,10},{26,18},{... | collective-permute-start | bytes 41480 | tf_op jit(solution)/shard_map/ppermute | solution.py:23
  16.9 7.4 %collective-permute-start.2 = (bf16[9,1,34,384]{3,2,1,0:T(8,128)(2,1)S(1)}, bf16[9,1,34,384]{3,2,1,0:T(8,128)(2,1)S(1)}, u32[]{:S(2)}, u32[]{:S(2)}) collective-permute-start(bf16[9,1,34,384]{3,2,1,0:T(8,128)(2,1)S(1)} %get-tuple-element.82), channel_id=1, source_target_pairs={{0,1},{1,2},{2,3},{3,4},{4,5},{5,6},{6,7},{8,9},{9,10},{10,11},{11... | collective-permute-start | bytes 705032 | tf_op jit(solution)/shard_map/ppermute | solution.py:22
  20.8 8.1 %collective-permute-start.3 = (bf16[9,1,34,384]{3,2,1,0:T(8,128)(2,1)S(1)}, bf16[9,1,34,384]{3,2,1,0:T(8,128)(2,1)S(1)}, u32[]{:S(2)}, u32[]{:S(2)}) collective-permute-start(bf16[9,1,34,384]{3,2,1,0:T(8,128)(2,1)S(1)} %get-tuple-element.83), channel_id=1, source_target_pairs={{1,0},{2,1},{3,2},{4,3},{5,4},{6,5},{7,6},{9,8},{10,9},{11,10},{12... | collective-permute-start | bytes 705032 | tf_op jit(solution)/shard_map/ppermute | solution.py:23
  38.2 1.2 copy-start.15
  39.4 6.2 %copy-start.1 = (bf16[3,3,384,192]{2,3,1,0:T(8,128)(2,1)S(1)}, bf16[3,3,384,192]{2,3,1,0:T(8,128)(2,1)}, u32[]{:S(2)}) copy-start(bf16[3,3,384,192]{2,3,1,0:T(8,128)(2,1)} %param.16) | copy-start | bytes 3981316
  39.8 13.3 %collective-permute-start.4 = (bf16[9,2,1,384]{3,2,1,0:T(2,128)(2,1)S(1)}, bf16[9,2,1,384]{3,2,1,0:T(2,128)(2,1)S(1)}, u32[]{:S(2)}, u32[]{:S(2)}) collective-permute-start(bf16[9,2,1,384]{3,2,1,0:T(2,128)(2,1)S(1)} %get-tuple-element.92), channel_id=1, source_target_pairs={{0,8},{8,16},{16,24},{1,9},{9,17},{17,25},{2,10},{10,18},{18,26},{... | collective-permute-start | bytes 41480 | tf_op jit(solution)/shard_map/ppermute | solution.py:22
  44.1 9.1 %collective-permute-start.5 = (bf16[9,2,1,384]{3,2,1,0:T(2,128)(2,1)S(1)}, bf16[9,2,1,384]{3,2,1,0:T(2,128)(2,1)S(1)}, u32[]{:S(2)}, u32[]{:S(2)}) collective-permute-start(bf16[9,2,1,384]{3,2,1,0:T(2,128)(2,1)S(1)} %get-tuple-element.93), channel_id=1, source_target_pairs={{8,0},{16,8},{24,16},{9,1},{17,9},{25,17},{10,2},{18,10},{26,18},{... | collective-permute-start | bytes 41480 | tf_op jit(solution)/shard_map/ppermute | solution.py:23
  52.7 5.1 %copy-start.9 = (bf16[1,1,3,384,384]{4,3,2,1,0:T(8,128)(2,1)S(1)}, bf16[1,1,3,384,384]{4,3,2,1,0:T(8,128)(2,1)}, u32[]{:S(2)}) copy-start(bf16[1,1,3,384,384]{4,3,2,1,0:T(8,128)(2,1)} %get-tuple-element.10) | copy-start | bytes 2654212
  53.5 5.5 %collective-permute-start.6 = (bf16[9,1,34,384]{3,2,1,0:T(8,128)(2,1)S(1)}, bf16[9,1,34,384]{3,2,1,0:T(8,128)(2,1)S(1)}, u32[]{:S(2)}, u32[]{:S(2)}) collective-permute-start(bf16[9,1,34,384]{3,2,1,0:T(8,128)(2,1)S(1)} %get-tuple-element.80), channel_id=1, source_target_pairs={{0,1},{1,2},{2,3},{3,4},{4,5},{5,6},{6,7},{8,9},{9,10},{10,11},{11... | collective-permute-start | bytes 705032 | tf_op jit(solution)/shard_map/ppermute | solution.py:22
  55.5 8.7 %collective-permute-start.7 = (bf16[9,1,34,384]{3,2,1,0:T(8,128)(2,1)S(1)}, bf16[9,1,34,384]{3,2,1,0:T(8,128)(2,1)S(1)}, u32[]{:S(2)}, u32[]{:S(2)}) collective-permute-start(bf16[9,1,34,384]{3,2,1,0:T(8,128)(2,1)S(1)} %get-tuple-element.81), channel_id=1, source_target_pairs={{1,0},{2,1},{3,2},{4,3},{5,4},{6,5},{7,6},{9,8},{10,9},{11,10},{12... | collective-permute-start | bytes 705032 | tf_op jit(solution)/shard_map/ppermute | solution.py:23
  67.1 1.2 copy-start.8
  77.3 5.6 %collective-permute-start.8 = (bf16[2,1,384]{2,1,0:T(2,128)(2,1)S(1)}, bf16[2,1,384]{2,1,0:T(2,128)(2,1)S(1)}, u32[]{:S(2)}, u32[]{:S(2)}) collective-permute-start(bf16[2,1,384]{2,1,0:T(2,128)(2,1)S(1)} %get-tuple-element.109), channel_id=1, source_target_pairs={{0,8},{8,16},{16,24},{1,9},{9,17},{17,25},{2,10},{10,18},{18,26},{... | collective-permute-start | bytes 4616 | tf_op jit(solution)/shard_map/ppermute | solution.py:22
  81.6 4.3 %collective-permute-start.9 = (bf16[2,1,384]{2,1,0:T(2,128)(2,1)S(1)}, bf16[2,1,384]{2,1,0:T(2,128)(2,1)S(1)}, u32[]{:S(2)}, u32[]{:S(2)}) collective-permute-start(bf16[2,1,384]{2,1,0:T(2,128)(2,1)S(1)} %get-tuple-element.110), channel_id=1, source_target_pairs={{8,0},{16,8},{24,16},{9,1},{17,9},{25,17},{10,2},{18,10},{26,18},{... | collective-permute-start | bytes 4616 | tf_op jit(solution)/shard_map/ppermute | solution.py:23
  86.0 9.5 %collective-permute-start.10 = (bf16[1,34,384]{2,1,0:T(8,128)(2,1)S(1)}, bf16[1,34,384]{2,1,0:T(8,128)(2,1)S(1)}, u32[]{:S(2)}, u32[]{:S(2)}) collective-permute-start(bf16[1,34,384]{2,1,0:T(8,128)(2,1)S(1)} %get-tuple-element.107), channel_id=1, source_target_pairs={{0,1},{1,2},{2,3},{3,4},{4,5},{5,6},{6,7},{8,9},{9,10},{10,11},{11... | collective-permute-start | bytes 78344 | tf_op jit(solution)/shard_map/ppermute | solution.py:22
  89.2 6.3 %collective-permute-start.11 = (bf16[1,34,384]{2,1,0:T(8,128)(2,1)S(1)}, bf16[1,34,384]{2,1,0:T(8,128)(2,1)S(1)}, u32[]{:S(2)}, u32[]{:S(2)}) collective-permute-start(bf16[1,34,384]{2,1,0:T(8,128)(2,1)S(1)} %get-tuple-element.108), channel_id=1, source_target_pairs={{1,0},{2,1},{3,2},{4,3},{5,4},{6,5},{7,6},{9,8},{10,9},{11,10},{12... | collective-permute-start | bytes 78344 | tf_op jit(solution)/shard_map/ppermute | solution.py:23
  91.9 14.9 %all-to-all-start = ((bf16[4,2,2,32,384]{4,3,2,1,0:T(8,128)(2,1)}), bf16[4,2,2,32,384]{4,3,2,1,0:T(8,128)(2,1)S(1)}, u32[]{:S(2)}, u32[]{:S(2)}) async-start(bf16[4,2,2,32,384]{4,3,2,1,0:T(8,128)(2,1)} %pad_maximum_fusion.9), calls=%async_computation | async-start | bytes 786432 | tf_op jit(solution)/shard_map/all_to_all | solution.py:11
  97.3 16.8 %copy-start.18 = (f32[192]{0:T(256)S(1)}, f32[192]{0:T(256)}, u32[]{:S(2)}) copy-start(f32[192]{0:T(256)} %param.17) | copy-start | bytes 2308
  106.9 8.2 %collective-permute-start.12 = (bf16[2,1,128,384]{3,2,1,0:T(8,128)(2,1)S(1)}, bf16[2,1,128,384]{3,2,1,0:T(8,128)(2,1)S(1)}, u32[]{:S(2)}, u32[]{:S(2)}) collective-permute-start(bf16[2,1,128,384]{3,2,1,0:T(8,128)(2,1)S(1)} %get-tuple-element.96), channel_id=1, source_target_pairs={{0,1},{1,2},{2,3},{3,4},{4,5},{5,6},{6,7},{8,9},{9,10},{10,11},{11... | collective-permute-start | bytes 589832 | tf_op jit(solution)/shard_map/ppermute | solution.py:22
  112.0 7.0 %collective-permute-start.13 = (bf16[2,1,128,384]{3,2,1,0:T(8,128)(2,1)S(1)}, bf16[2,1,128,384]{3,2,1,0:T(8,128)(2,1)S(1)}, u32[]{:S(2)}, u32[]{:S(2)}) collective-permute-start(bf16[2,1,128,384]{3,2,1,0:T(8,128)(2,1)S(1)} %get-tuple-element.97), channel_id=1, source_target_pairs={{1,0},{2,1},{3,2},{4,3},{5,4},{6,5},{7,6},{9,8},{10,9},{11,10},{12... | collective-permute-start | bytes 589832 | tf_op jit(solution)/shard_map/ppermute | solution.py:23
  132.5 2.2 %copy-start.10 = (bf16[1152,192,1,1]{0,1,2,3:T(8,128)(2,1)S(1)}, bf16[1152,192,1,1]{0,1,2,3:T(8,128)(2,1)}, u32[]{:S(2)}) copy-start(bf16[1152,192,1,1]{0,1,2,3:T(8,128)(2,1)} %reshape.105) | copy-start | bytes 1327108
  134.8 2.3 %copy-start.11 = (bf16[1152,192,1,1]{0,1,2,3:T(8,128)(2,1)S(1)}, bf16[1152,192,1,1]{0,1,2,3:T(8,128)(2,1)}, u32[]{:S(2)}) copy-start(bf16[1152,192,1,1]{0,1,2,3:T(8,128)(2,1)} %reshape.107) | copy-start | bytes 1327108
  (12 other events, 13.1 us)
